TPU v7x, 512 devices: a whole 4x4x16 slice. The times are simulated.
512 devices in a mesh: ctx: 32 (over z, core), exp: 16 (over y, x).
Axes of the slice: x: 4, y: 4, z: 16, core: 2. Of those that a mesh axis runs over, the one named last changes fastest.
Arguments:
- ssm_input: bfloat16 [4096, 8192], P('ctx', 'exp'), may hold values from -6 to 6
- gate_input: bfloat16 [4096, 8192], P('ctx', 'exp'), may hold values from -6 to 6
- state_in_proj: bfloat16 [4096, 128], P('ctx'), may hold values from -0.29882812 to 0.29882812
- state_out_proj: bfloat16 [4096, 128], P('ctx'), may hold values from -0.5 to 0.5
- log_decay: float32 [4096, 128], P('ctx', 'exp'), as said below
- skip_gain: float32 [128], P('exp'), may hold values from 0.5 to 1.5
- out_weight: bfloat16 [8192, 4096], P('exp', 'ctx'), may hold values from -0.0625 to 0.0625
- routes: int32 [4096, 2], replicated, may hold values from 0 to 15, all different within a row; in each aligned block of 8 rows (0 to 7, 8 to 15, ...) at most 2 rows name the same one
- route_weights: bfloat16 [4096, 2], replicated, may hold values from 0.099609375 to 1
- expert_gate: bfloat16 [16, 4096, 12288], P('exp', None, 'ctx'), may hold values from -0.09375 to 0.09375
Outputs:
- gate_act: bfloat16 [16, 1024, 12288], P('exp', None, 'ctx')
Inputs may be any that keep to these rules, and one draw needn't show every extreme that they name: `routes`: each row names 2 different experts, every expert is named by some row, and in each aligned block of 8 rows no expert is named by more than 2 rows. `log_decay`: every entry is negative.
All inputs are finite; a program needn't handle non-finite values.
Results may differ from a plain program's by a relative error of at most 0.025.
Values may be sent and summed in bfloat16 or wider, within the bound.
A program may use at most 128 MiB of HBM per device.

v0:
```python
from functools import partial

import jax
import jax.numpy as jnp
from jax import lax
from jax.sharding import PartitionSpec as P


def entering(shard, axis, combine, identity):
    peers, index = (lax.axis_size(axis), lax.axis_index(axis))
    everything = jax.tree.map(
        lambda part, kind: lax.all_gather(part.astype(kind), axis),
        shard,
        (jnp.bfloat16, jnp.bfloat16),
    )
    start = jax.tree.map(
        lambda part, zero: jnp.broadcast_to(jnp.asarray(zero, part.dtype), part.shape),
        shard,
        identity,
    )

    def step(k, before):
        reached = k < index
        new = combine(
            before, jax.tree.map(lambda part, own: part[k].astype(own.dtype), everything, shard)
        )
        return jax.tree.map(lambda a, b: jnp.where(reached, a, b), new, before)

    return lax.fori_loop(0, peers, step, start)


def slot_masks(route_block, expert_count, capacity):
    flat_ids = route_block.reshape(-1)
    onehot = (flat_ids[:, None] == jnp.arange(expert_count, dtype=jnp.int32)[None, :]).astype(
        jnp.int32
    )
    earlier_count = jnp.sum((jnp.cumsum(onehot, axis=0) - onehot) * onehot, axis=1)
    slot_index = flat_ids * capacity + earlier_count
    matches = (
        slot_index[None, :] == jnp.arange(expert_count * capacity, dtype=jnp.int32)[:, None]
    ).astype(jnp.int32)
    shaped = matches.reshape(expert_count * capacity, route_block.shape[0], route_block.shape[1])
    return jnp.sum(shaped, axis=2).astype(jnp.bfloat16)


def owner_weights(routes, route_weights, sources, own_expert, capacity):
    per_source = routes.reshape(sources, -1)
    weights_flat = route_weights.astype(jnp.float32).reshape(sources, -1)
    hits = (per_source == own_expert).astype(jnp.int32)
    place = jnp.cumsum(hits, axis=1) - hits
    chosen = (place[:, :, None] == jnp.arange(capacity, dtype=jnp.int32)[None, None, :]) & (
        hits[:, :, None] > 0
    )
    return jnp.sum(jnp.where(chosen, weights_flat[:, :, None], 0.0), axis=1).reshape(-1)


def body(
    ssm_input,
    gate_input,
    state_in_proj,
    state_out_proj,
    log_decay,
    skip_gain,
    out_weight,
    routes,
    route_weights,
    expert_gate,
):
    highest = lax.Precision.HIGHEST
    tokens = ssm_input.shape[0]
    head_count = log_decay.shape[1]
    head_width = ssm_input.shape[1] // head_count
    inputs = ssm_input.astype(jnp.float32).reshape(tokens, head_count, head_width)
    cumulative = jnp.cumsum(log_decay, axis=0)
    scores = jnp.dot(state_out_proj, state_in_proj.T, preferred_element_type=jnp.float32)
    position = lax.broadcasted_iota(jnp.int32, (tokens, tokens), 0)
    anchor = lax.broadcasted_iota(jnp.int32, (tokens, tokens), 1)
    causal = (position >= anchor)[:, :, None]
    log_gaps = jnp.where(causal, cumulative[:, None, :] - cumulative[None, :, :], 0.0)
    mixing = jnp.where(causal, jnp.exp(log_gaps), 0.0) * scores[:, :, None]
    within = jnp.einsum("tsh,shp->thp", mixing, inputs, precision=highest)
    to_end = jnp.exp(cumulative[-1][None, :] - cumulative)
    local_state = jnp.einsum(
        "sh,shp,sn->hpn", to_end, inputs, state_in_proj.astype(jnp.float32), precision=highest
    )
    span_decay = jnp.exp(cumulative[-1])

    def combine(earlier, latter):
        return (earlier[0] * latter[0], latter[0][:, None, None] * earlier[1] + latter[1])

    carried = entering(
        (span_decay, local_state),
        "ctx",
        combine,
        (jnp.ones_like(span_decay), jnp.zeros_like(local_state)),
    )
    from_before = (
        jnp.einsum("tn,hpn->thp", state_out_proj.astype(jnp.float32), carried[1], precision=highest)
        * jnp.exp(cumulative)[:, :, None]
    )
    overall = within + from_before + skip_gain[None, :, None] * inputs
    gated_out = (overall.reshape(tokens, -1) * jax.nn.silu(gate_input.astype(jnp.float32))).astype(
        jnp.bfloat16
    )
    partial_sums = jnp.dot(
        gated_out,
        lax.all_gather(out_weight, "ctx", axis=1, tiled=True),
        preferred_element_type=jnp.float32,
    )
    mixed_rows = lax.psum_scatter(
        partial_sums.astype(jnp.bfloat16), "exp", scatter_dimension=0, tiled=True
    )
    expert_count = lax.axis_size("exp")
    spans = lax.axis_size("ctx")
    block_rows = mixed_rows.shape[0]
    model_width = mixed_rows.shape[1]
    capacity = max(2, 4 * tokens // (expert_count * expert_count))
    sources = spans * expert_count
    own_expert = lax.axis_index("exp")
    row_weights = owner_weights(routes, route_weights, sources, own_expert, capacity)
    gate_local = expert_gate[0]
    route_blocks = routes.reshape(sources, block_rows, routes.shape[1])
    gathered = lax.all_gather(mixed_rows, "ctx", axis=0, tiled=True)
    grouped = route_blocks.reshape(spans, expert_count, block_rows, routes.shape[1])
    mine = lax.dynamic_index_in_dim(grouped, own_expert, 1, keepdims=False)
    masks = jax.vmap(partial(slot_masks, expert_count=expert_count, capacity=capacity))(mine)
    outgoing = jnp.einsum(
        "cer,crd->ced",
        masks,
        gathered.reshape(spans, block_rows, model_width),
        preferred_element_type=jnp.float32,
    )
    outgoing = outgoing.astype(jnp.bfloat16).reshape(spans, expert_count, capacity, model_width)
    arrived = lax.all_to_all(outgoing, "exp", split_axis=1, concat_axis=1, tiled=True)
    product = jnp.dot(
        arrived.reshape(-1, model_width), gate_local, preferred_element_type=jnp.float32
    )
    activation = (row_weights[:, None] * jax.nn.silu(product)).astype(jnp.bfloat16)
    return activation[None]


def solution(mesh):
    in_specs = (
        P("ctx", "exp"),
        P("ctx", "exp"),
        P("ctx", None),
        P("ctx", None),
        P("ctx", "exp"),
        P("exp"),
        P("exp", "ctx"),
        P(),
        P(),
        P("exp", None, "ctx"),
    )
    out_specs = P("exp", None, "ctx")
    return jax.shard_map(body, mesh=mesh, in_specs=in_specs, out_specs=out_specs, check_vma=False)
```

profile of v0, /device:TPU:1, one launch (start us, length us, event | category | flops | bytes accessed | tf_op | source)
XLA Modules:
  0.0 561.3 jit_solution(13182349372676830319)
XLA Ops:
  9.4 1.7 convolution_convert_fusion.2
  13.2 37.3 %all-gather.1 = bf16[32,1,8]{2,1,0:T(2,128)(2,1)S(1)} all-gather(bf16[1,1,8]{2,1,0:T(2,128)(2,1)S(1)} %get-tuple-element.161), channel_id=1, replica_groups=mesh['ctx'=32,'exp'=16] {'ctx'}, dimensions={0}, use_global_device_ids=true | all-gather | bytes 528 | tf_op jit(solution)/shard_map/all_gather | solution.py:12
  51.5 1.6 fusion.41
  53.0 38.2 %all-gather.10.cloned.1.call-done = bf16[256,64,128]{2,1,0:T(8,128)(2,1)} async-done(((bf16[8,64,128]{2,1,0:T(8,128)(2,1)}), bf16[256,64,128]{2,1,0:T(8,128)(2,1)}) %all-gather.10.cloned.1.call-update) | async-done | bytes 4194320 | tf_op jit(solution)/shard_map/all_gather | solution.py:12
  91.2 33.7 %while.14 = (s32[]{:T(128)}, f32[8,64,128]{2,1,0:T(8,128)S(1)}, s32[]{:T(128)}, bf16[32,8]{1,0:T(8,128)(2,1)S(1)}, bf16[32,8,64,128]{3,2,1,0:T(8,128)(2,1)}, /*index=5*/s32[]{:T(128)}, s32[]{:T(128)}) while((s32[]{:T(128)}, f32[8,64,128]{2,1,0:T(8,128)S(1)}, s32[]{:T(128)}, bf16[32,8]{1,0:T(8,128)(2,1)S(1)}, ...), condition=%wide.region_7.8_spmd.clone, body=%wide.region_6.7_spmd.clone.sunk | while | flops 327692 | bytes 655545 | solution.py:29
  126.0 2.3 fusion.11
  129.4 40.5 %all-gather.6.cloned.1.call-done = bf16[512,4096]{1,0:T(8,128)(2,1)} async-done(((bf16[512,128]{1,0:T(8,128)(2,1)}), bf16[512,4096]{1,0:T(8,128)(2,1)}) %all-gather.6.cloned.1.call-update) | async-done | bytes 4194320 | tf_op jit(solution)/shard_map/all_gather | solution.py:107
  169.9 4.0 convolution_convert_fusion.1
  174.0 1.3 dynamic-slice
  175.9 110.5 %all-reduce.3.cloned.1.call-done = bf16[128,4096]{1,0:T(8,128)(2,1)} async-done(((bf16[128,4096]{1,0:T(8,128)(2,1)}), bf16[128,4096]{1,0:T(8,128)(2,1)}) %all-reduce.3.cloned.1.call-update) | async-done | bytes 1048592
  286.4 1.5 constant_dynamic-slice_fusion
  291.0 70.5 %all-gather.8.cloned.1.call-done = bf16[256,4096]{1,0:T(8,128)(2,1)} async-done(((bf16[8,4096]{1,0:T(8,128)(2,1)}), bf16[256,4096]{1,0:T(8,128)(2,1)}) %all-gather.8.cloned.1.call-update) | async-done | bytes 2097168 | tf_op jit(solution)/shard_map/all_gather | solution.py:123
  361.4 7.2 %convolution_convert_fusion = bf16[32,32,4096]{2,1,0:T(8,128)(2,1)} fusion(bf16[256,4096]{1,0:T(8,128)(2,1)} %all-gather.8.cloned.1.call-done, s32[32,32,8]{1,2,0:T(8,128)S(1)} %convert_reduce_fusion), kind=kOutput, calls=%fused_computation.3 | convolution fusion | flops 71311360 | bytes 10518528 | tf_op jit(solution)/shard_map/cer,crd->ced/dot_general | solution.py:127
  368.6 14.1 %reshape.93 = bf16[32,16,2,4096]{3,2,1,0:T(2,128)(2,1)} reshape(bf16[32,32,4096]{2,1,0:T(8,128)(2,1)} %convolution_convert_fusion) | data formatting | bytes 16777216 | tf_op jit(solution)/shard_map/reshape | solution.py:133
  382.7 9.1 %copy.133 = bf16[32,16,2,4096]{3,2,0,1:T(2,128)(2,1)} copy(bf16[32,16,2,4096]{3,2,1,0:T(2,128)(2,1)} %reshape.93) | data formatting | bytes 16777216 | tf_op jit(solution)/shard_map/reshape | solution.py:133
  391.8 6.6 %all-to-all-start = ((bf16[32,16,2,4096]{3,2,0,1:T(2,128)(2,1)}), bf16[32,16,2,4096]{3,2,0,1:T(2,128)(2,1)}, u32[]{:S(2)}, u32[]{:S(2)}) async-start(bf16[32,16,2,4096]{3,2,0,1:T(2,128)(2,1)} %copy.133), calls=%async_computation | async-start | bytes 16777216 | tf_op jit(solution)/shard_map/all_to_all | solution.py:134
  398.5 2.0 copy.113
  400.5 2.2 reshape.97
  403.0 1.8 copy.117
  404.7 2.2 reshape.98
  407.4 116.0 %all-to-all-done = bf16[32,16,2,4096]{3,2,0,1:T(2,128)(2,1)} async-done(((bf16[32,16,2,4096]{3,2,0,1:T(2,128)(2,1)}), bf16[32,16,2,4096]{3,2,0,1:T(2,128)(2,1)}, u32[]{:S(2)}, u32[]{:S(2)}) %all-to-all-start) | async-done | bytes 8388640 | tf_op jit(solution)/shard_map/all_to_all | solution.py:134
  523.4 9.4 %copy.134 = bf16[32,16,2,4096]{3,2,1,0:T(2,128)(2,1)} copy(bf16[32,16,2,4096]{3,2,0,1:T(2,128)(2,1)} %all-to-all-done) | data formatting | bytes 16777216 | tf_op jit(solution)/shard_map/all_to_all | solution.py:134
  532.7 13.1 %reshape.94 = bf16[1024,4096]{1,0:T(8,128)(2,1)} reshape(bf16[32,16,2,4096]{3,2,1,0:T(2,128)(2,1)} %copy.134) | data formatting | bytes 16777216 | tf_op jit(solution)/shard_map/reshape | solution.py:136
  545.8 8.9 %fusion.6 = bf16[1,1024,384]{2,1,0:T(8,128)(2,1)} fusion(bf16[1024,4096]{1,0:T(8,128)(2,1)} %reshape.94, bf16[1,4096,384]{2,1,0:T(8,128)(2,1)S(1)} %copy-done, f32[1024]{0:T(1024)S(1)} %mul.83), kind=kOutput, calls=%fused_computation.9 | convolution fusion | flops 3223584768 | bytes 12324864 | tf_op jit(solution)/shard_map/dot_general | solution.py:135
  (113 shorter events, 44.6 us)
Async XLA Ops:
  6.5 539.3 %copy-start = (bf16[1,4096,384]{2,1,0:T(8,128)(2,1)S(1)}, bf16[1,4096,384]{2,1,0:T(8,128)(2,1)}, u32[]{:S(2)}) copy-start(bf16[1,4096,384]{2,1,0:T(8,128)(2,1)} %param.21) | copy-start | bytes 9437188
  6.5 84.6 %all-gather.10.cloned.1.call-start = ((), (), s32[]{:S(2)}) async-start(), calls=%async_computation.3 | async-start | bytes 4325376 | tf_op jit(solution)/shard_map/all_gather | solution.py:12
  9.4 2.5 copy-start.1
  11.1 158.8 %all-gather.6.cloned.1.call-start = ((), (), s32[]{:S(2)}) async-start(), calls=%async_computation.1 | async-start | bytes 4325376 | tf_op jit(solution)/shard_map/all_gather | solution.py:107
  11.9 274.5 %all-reduce.3.cloned.1.call-start = ((), (), s32[]{:S(2)}) async-start(), calls=%async_computation.4 | async-start | bytes 2097152
  12.6 113.3 %copy-start.2 = (bf16[128,512]{0,1:T(8,128)(2,1)S(1)}, bf16[128,512]{0,1:T(8,128)(2,1)}, u32[]{:S(2)}) copy-start(bf16[128,512]{0,1:T(8,128)(2,1)} %copy-done.1) | copy-start | bytes 393220
  129.4 158.5 %copy-start.3 = (s32[4096,2]{0,1:T(2,128)S(1)}, s32[4096,2]{0,1:T(2,128)}, u32[]{:S(2)}) copy-start(s32[4096,2]{0,1:T(2,128)} %param.19) | copy-start | bytes 98308
  173.9 187.5 %all-gather.8.cloned.1.call-start = ((), (), s32[]{:S(2)}) async-start(), calls=%async_computation.2 | async-start | bytes 2162688 | tf_op jit(solution)/shard_map/all_gather | solution.py:123
  391.8 131.5 %all-to-all-start = ((bf16[32,16,2,4096]{3,2,0,1:T(2,128)(2,1)}), bf16[32,16,2,4096]{3,2,0,1:T(2,128)(2,1)}, u32[]{:S(2)}, u32[]{:S(2)}) async-start(bf16[32,16,2,4096]{3,2,0,1:T(2,128)(2,1)} %copy.133), calls=%async_computation | async-start | bytes 16777216 | tf_op jit(solution)/shard_map/all_to_all | solution.py:134
  398.4 4.5 copy-start.4
Sparse Core Ops, SparseCore 0:
  11.3 79.8 all-gather.9
  93.2 76.6 all-gather.5
  174.0 112.3 all-reduce.2
  288.4 72.9 all-gather.7
where the time goes:
time: 563 us; the launch traced here: 561 us
  waiting for transfers between devices  376 us (67%)
  local copies, waits for them, and re-layouts  64.1 us (11%)
  blocking collectives  37.3 us (7%)
  other arithmetic  35.1 us (6%)
  matrix products  26.7 us (5%)
  between operations  14 us (2%)
  starting transfers between devices  6.71 us (1%)
    all_to_all x1, waiting for transfers between devices, body(): lax.all_to_all(outgoing, 'exp', split_axis=1, concat_axis=1, tiled=True)  116 us
    unnamed x5, waiting for transfers between devices  111 us
    all_gather x1, waiting for transfers between devices, body(): gathered = lax.all_gather(mixed_rows, 'ctx', axis=0, tiled=True)  70.5 us
    all_gather x1, waiting for transfers between devices, body(): lax.all_gather(out_weight, 'ctx', axis=1, tiled=True)  40.5 us
    all_gather x1, waiting for transfers between devices, entering(): lax.all_gather(part.astype(kind), axis)  38.2 us
    all_gather x1, blocking collectives, entering(): lax.all_gather(part.astype(kind), axis)  37.3 us
    select_n x32, other arithmetic, step(): return jax.tree.map(lambda a, b: jnp.where(reached, a, b), new, before)  32.4 us
    reshape x2, local copies, waits for them, and re-layouts, body(): outgoing.astype(jnp.bfloat16)  23.2 us
  transfers between devices with their start and end apart: 5, of which 5 were waited for; matrix products, arithmetic and copies ran while one was open for 10% of the time, Pallas kernels for 0%

commit v1 on v0

v1 whole, which is shorter than its diff:
```python
import jax
import jax.numpy as jnp
from jax import lax
from jax.experimental import pallas as pl
from jax.experimental.pallas import tpu as pltpu
from jax.sharding import PartitionSpec as P

MESH = pl.DeviceIdType.MESH
SOURCE = 8
CAP = 2
FLOOR = -110.0
HIGHEST = lax.Precision.HIGHEST
WQ = 4
AQ = 2
bf16 = jnp.bfloat16
f32 = jnp.float32


def dot(a, b, dims=((1,), (0,)), precision=None):
    return lax.dot_general(a, b, (dims, ((), ())), preferred_element_type=f32, precision=precision)


def iota(shape, dim):
    return lax.broadcasted_iota(jnp.int32, shape, dim)


def silu(v):
    return v / (1.0 + jnp.exp(-v))


def kernel(
    x_ref, gt_ref, b_ref, c_ref, ld_ref, skip_ref, w_hbm, r_ref, rw_ref, g_hbm,
    out_ref,
    wbuf, abuf, gbuf, psend, precv, dsend, stb, dec, rs, rd, pre, carr,
    g_sem, w_sem, s1_send, s1_recv, d1_send, d1_recv, s2_send, s2_recv,
    w_send, w_recv, ws_send, ws_recv, p_send, p_recv, m_send, m_recv, a_send, a_recv, as_send, as_recv,
):
    nc, ne = lax.axis_size("ctx"), lax.axis_size("exp")
    nz = nc // 2
    up, down = nz // 2, nz - 1 - nz // 2
    c, e = lax.axis_index("ctx"), lax.axis_index("exp")
    z, core = c // 2, c % 2
    tokens, width = x_ref.shape
    heads = ld_ref.shape[1]
    hw = width // heads
    cols = psend.shape[2]

    def at_z(chip, lane):
        return {"ctx": lax.rem(chip + nz, nz) * 2 + lane}

    barrier = pltpu.get_barrier_semaphore()
    for k in range(1, nc):
        pl.semaphore_signal(barrier, 1, device_id={"ctx": lax.rem(c + k, nc)}, device_id_type=MESH)
    for k in range(1, ne):
        pl.semaphore_signal(barrier, 1, device_id={"exp": lax.rem(e + k, ne)}, device_id_type=MESH)

    load_g = pltpu.make_async_copy(g_hbm.at[0], gbuf, g_sem)
    load_w = pltpu.make_async_copy(w_hbm, wbuf.at[c], w_sem)
    load_w.start()
    load_g.start()

    ld = jnp.maximum(ld_ref[...], FLOOR)
    row, col = iota((tokens, tokens), 0), iota((tokens, tokens), 1)
    causal = row >= col
    cum = dot(causal.astype(f32), ld, precision=HIGHEST)
    cum_t = dot(ld, (row <= col).astype(f32), ((0,), (0,)), HIGHEST)
    spread = (iota((heads, width), 1) // hw == iota((heads, width), 0)).astype(f32)
    cum_x = dot(cum, spread, precision=HIGHEST)
    x = x_ref[...]
    xf = x.astype(f32)
    span = jnp.exp(cum_x[tokens - 1 :, :])
    to_end = jnp.exp(cum_x[tokens - 1 :, :] - cum_x)
    local = dot(b_ref[...], (xf * to_end).astype(bf16), ((0,), (0,))).astype(bf16)
    lane_blocks = width // 128
    for j in range(nc):
        rb, lb = j // lane_blocks, j % lane_blocks
        stb[j] = local[rb * 16 : (rb + 1) * 16, lb * 128 : (lb + 1) * 128]
    for lb in range(lane_blocks):
        dec[lb] = span[:, lb * 128 : (lb + 1) * 128]

    pl.semaphore_wait(barrier, nc - 1 + ne - 1)

    def s1(j):
        return pltpu.make_async_remote_copy(
            stb.at[j], rs.at[c], s1_send, s1_recv, device_id={"ctx": j}, device_id_type=MESH)

    def d1(j):
        return pltpu.make_async_remote_copy(
            dec.at[lax.rem(j, lane_blocks)], rd.at[c], d1_send, d1_recv, device_id={"ctx": j}, device_id_type=MESH)

    def s2(j):
        place = carr.at[pl.ds(pl.multiple_of(c // lane_blocks * 16, 16), 16), pl.ds(pl.multiple_of(c % lane_blocks * 128, 128), 128)]
        return pltpu.make_async_remote_copy(
            pre.at[j], place, s2_send, s2_recv, device_id={"ctx": j}, device_id_type=MESH)

    def await_bytes(ref, sem):
        pltpu.make_async_copy(ref, ref, sem).wait()

    wrows = wbuf.shape[1] // WQ

    def w_piece(chip, lane, q):
        return wbuf.at[lax.rem(chip + nz, nz) * 2 + lane, pl.ds(q * wrows, wrows), :]

    def w_hop(dd, i, q):
        turn = 1 - 2 * dd
        piece = w_piece(z - turn * i, core, q)
        return pltpu.make_async_remote_copy(
            piece, piece, w_send, w_recv.at[dd, i, q], device_id=at_z(z + turn, core), device_id_type=MESH)

    def w_arrived(dd, i, q):
        piece = w_piece(z - (1 - 2 * dd) * (i + 1), core, q)
        pltpu.make_async_copy(piece, piece, w_recv.at[dd, i, q]).wait()

    def w_side(chip):
        chip = lax.rem(chip + nz, nz)
        block = wbuf.at[chip * 2 + core]
        return pltpu.make_async_remote_copy(
            block, block, ws_send, ws_recv.at[chip], device_id={"ctx": c + 1 - 2 * core}, device_id_type=MESH)

    def w_step(i):
        for q in range(WQ):
            for dd, hops in ((0, up), (1, down)):
                if 0 < i <= hops:
                    w_arrived(dd, i - 1, q)
                if i < hops:
                    w_hop(dd, i, q).start()
        if i == 0:
            w_side(z).start()
        else:
            for dd, hops in ((0, up), (1, down)):
                if i <= hops:
                    w_side(z - (1 - 2 * dd) * i).start()

    load_w.wait()
    for k in range(1, nc):
        s1(lax.rem(c + k, nc)).start()
        d1(lax.rem(c + k, nc)).start()
    w_step(0)
    rs[pl.ds(c, 1)] = stb[pl.ds(c, 1)]
    rd[pl.ds(c, 1)] = dec[pl.ds(lax.rem(c, lane_blocks), 1)]

    scores = dot(c_ref[...], b_ref[...], ((1,), (1,)))
    pairs = []
    for p in range(width // 128):
        xp = x[:, p * 128 : (p + 1) * 128]
        part = None
        for h in range(p * 128 // hw, (p + 1) * 128 // hw):
            gap = jnp.minimum(cum[:, h : h + 1] - cum_t[h : h + 1, :], 0.0)
            mixing = (jnp.where(causal, jnp.exp(gap), 0.0) * scores).astype(bf16)
            y = dot(mixing, xp)
            part = y if part is None else jnp.where(iota(y.shape, 1) // hw == h - p * 128 // hw, y, part)
        pairs.append(part)
    skip = dot(skip_ref[...], spread, precision=HIGHEST)
    within = jnp.concatenate(pairs, axis=1) + skip * xf

    same = (row // SOURCE == col // SOURCE) & (row < col)
    before = same.astype(bf16)
    r0, r1 = r_ref[0, pl.ds(c, 1), :], r_ref[1, pl.ds(c, 1), :]
    experts = iota((ne, tokens), 0)
    hit = (r0 == experts) | (r1 == experts)
    pos = dot(hit.astype(bf16), before)
    slots = tokens // SOURCE * CAP
    target = jnp.where(hit, (iota((ne, tokens), 1) // SOURCE) * CAP + pos.astype(jnp.int32), -1)
    masks = (target[:, None, :] == iota((ne, slots, tokens), 1)).astype(f32).astype(bf16).reshape(ne * slots, tokens)
    own0, own1 = (r_ref[0] == e), (r_ref[1] == e)
    own = own0 | own1
    own_pos = dot(own.astype(bf16), before)
    own_target = jnp.where(own, (iota((nc, tokens), 1) // SOURCE) * CAP + own_pos.astype(jnp.int32), -1)
    own_weight = jnp.where(own0, rw_ref[0], jnp.where(own1, rw_ref[1], 0.0))

    w_step(1)
    w_step(2)

    await_bytes(rs.at[pl.ds(0, nc - 1)], s1_recv)
    await_bytes(rd.at[pl.ds(0, nc - 1)], d1_recv)
    state = jnp.zeros(rs.shape[1:], f32)
    for j in range(nc):
        pre[j] = state.astype(bf16)
        state = rd[j] * state + rs[j].astype(f32)
    for k in range(1, nc):
        s2(lax.rem(c + k, nc)).start()
    carr[pl.ds(pl.multiple_of(c // lane_blocks * 16, 16), 16), pl.ds(pl.multiple_of(c % lane_blocks * 128, 128), 128)] = pre[c]

    w_step(3)
    w_step(4)

    await_bytes(pre.at[pl.ds(0, nc - 1)], s2_recv)
    from_before = dot(c_ref[...], carr[...]) * jnp.exp(cum_x)
    gated = ((within + from_before) * silu(gt_ref[...].astype(f32))).astype(bf16)

    for i in range(5, up + 1):
        w_step(i)
    for k in range(nz):
        block = wbuf.at[k * 2 + 1 - core]
        pltpu.make_async_copy(block, block, ws_recv.at[k]).wait()

    def p_copy(j):
        return pltpu.make_async_remote_copy(
            psend.at[j], precv.at[e], p_send, p_recv, device_id={"exp": j}, device_id_type=MESH)

    shards = cols // 128

    def project(k, _):
        j = lax.rem(e + k, ne)
        for s in range(shards):
            psend[j, :, s * 128 : (s + 1) * 128] = dot(gated, wbuf[j * shards + s]).astype(bf16)

        @pl.when(k < ne)
        def _():
            p_copy(j).start()

        return 0

    lax.fori_loop(1, ne + 1, project, 0)
    precv[pl.ds(e, 1)] = psend[pl.ds(e, 1)]
    await_bytes(psend.at[pl.ds(0, ne - 1)], p_recv)
    total = precv[0].astype(f32)
    for k in range(1, ne):
        total += precv[k].astype(f32)
    mixed = total.astype(bf16)

    def m_copy(j):
        return pltpu.make_async_remote_copy(
            dsend.at[j], abuf.at[c, :, pl.ds(pl.multiple_of(e * cols, cols), cols)], m_send, m_recv,
            device_id={"exp": j}, device_id_type=MESH)

    dsend[...] = dot(masks, mixed).astype(bf16).reshape(dsend.shape)
    for k in range(1, ne):
        m_copy(lax.rem(e + k, ne)).start()
    abuf[pl.ds(c, 1), :, pl.ds(pl.multiple_of(e * cols, cols), cols)] = dsend[pl.ds(e, 1)]
    load_g.wait()
    await_bytes(dsend.at[pl.ds(0, ne - 1)], m_recv)

    arows = abuf.shape[1] // AQ

    def a_piece(chip, lane, q):
        return abuf.at[lax.rem(chip + nz, nz) * 2 + lane, pl.ds(q * arows, arows), :]

    def a_hop(dd, i, q):
        turn = 1 - 2 * dd
        piece = a_piece(z - turn * i, core, q)
        return pltpu.make_async_remote_copy(
            piece, piece, a_send, a_recv.at[dd, i, q], device_id=at_z(z + turn, core), device_id_type=MESH)

    def a_arrived(dd, i, q):
        piece = a_piece(z - (1 - 2 * dd) * (i + 1), core, q)
        pltpu.make_async_copy(piece, piece, a_recv.at[dd, i, q]).wait()

    def a_side(chip):
        block = abuf.at[chip * 2 + core]
        return pltpu.make_async_remote_copy(
            block, block, as_send, as_recv.at[chip], device_id={"ctx": c + 1 - 2 * core}, device_id_type=MESH)

    own_target = own_target.astype(f32)

    def expert(chip):
        block = abuf.at[chip * 2 + 1 - core]
        pltpu.make_async_copy(block, block, as_recv.at[chip]).wait()
        rows = abuf[pl.ds(chip * 2, 2)].reshape(2 * slots, abuf.shape[2])
        product = dot(rows, gbuf[...])
        weights = []
        for k in range(2):
            pick = iota((nc, tokens), 0) == chip * 2 + k
            goal = jnp.sum(jnp.where(pick, own_target, 0.0), axis=0, keepdims=True)
            value = jnp.sum(jnp.where(pick, own_weight, 0.0), axis=0, keepdims=True)
            at = goal == iota((slots, tokens), 0).astype(f32)
            weights.append(jnp.sum(jnp.where(at, value, 0.0), axis=1, keepdims=True))
        weight = jnp.concatenate(weights, axis=0)
        out_ref[0, pl.ds(pl.multiple_of(chip * 2 * slots, 2 * slots), 2 * slots), :] = (weight * silu(product)).astype(bf16)

    def a_step(i, _):
        for q in range(AQ):
            for dd, hops in ((0, up), (1, down)):

                @pl.when((i > 0) & (i <= hops))
                def _():
                    a_arrived(dd, i - 1, q)

                @pl.when(i < hops)
                def _():
                    a_hop(dd, i, q).start()

        for dd, hops in ((0, up), (1, down)):

            @pl.when((i <= hops) & ((i > 0) | (dd == 0)))
            def _():
                a_side(lax.rem(z - (1 - 2 * dd) * i + nz, nz)).start()

        for dd, hops in ((0, up), (1, down)):

            @pl.when((i > 0) & (i <= hops + 1) & ((i > 1) | (dd == 0)))
            def _():
                expert(lax.rem(z - (1 - 2 * dd) * (i - 1) + nz, nz))

        return 0

    lax.fori_loop(0, up + 2, a_step, 0)

    await_bytes(stb.at[pl.ds(0, nc - 1)], s1_send)
    await_bytes(rd.at[pl.ds(0, nc - 1)], d1_send)
    await_bytes(pre.at[pl.ds(0, nc - 1)], s2_send)
    await_bytes(wbuf.at[pl.ds(0, nz - 1)], w_send)
    await_bytes(wbuf.at[pl.ds(0, nz)], ws_send)
    await_bytes(psend.at[pl.ds(0, ne - 1)], p_send)
    await_bytes(dsend.at[pl.ds(0, ne - 1)], m_send)
    await_bytes(abuf.at[pl.ds(0, nz - 1)], a_send)
    await_bytes(abuf.at[pl.ds(0, nz)], as_send)


def body(x, gt, b, c, ld, skip, w, routes, weights, gate):
    nc, ne = lax.axis_size("ctx"), lax.axis_size("exp")
    tokens, width = x.shape
    heads = ld.shape[1]
    depth, shard = w.shape
    wide = shard * nc
    cols = wide // ne
    slots = tokens // SOURCE * CAP
    ff = gate.shape[2]
    lane_blocks = width // 128
    r = routes.T.reshape(2, nc, tokens)
    rw = weights.astype(f32).T.reshape(2, nc, tokens)
    vmem = pl.BlockSpec(memory_space=pltpu.VMEM)
    hbm = pl.BlockSpec(memory_space=pl.ANY)
    dma = pltpu.SemaphoreType.DMA
    return pl.pallas_call(
        kernel,
        out_shape=jax.ShapeDtypeStruct((1, nc * slots, ff), bf16),
        in_specs=[vmem] * 6 + [hbm] + [vmem] * 2 + [hbm],
        out_specs=vmem,
        scratch_shapes=[
            pltpu.VMEM((nc, depth, shard), bf16),
            pltpu.VMEM((nc, slots, wide), bf16),
            pltpu.VMEM((wide, ff), bf16),
            pltpu.VMEM((ne, tokens, cols), bf16),
            pltpu.VMEM((ne, tokens, cols), bf16),
            pltpu.VMEM((ne, slots, cols), bf16),
            pltpu.VMEM((nc, 16, 128), bf16),
            pltpu.VMEM((lane_blocks, 1, 128), f32),
            pltpu.VMEM((nc, 16, 128), bf16),
            pltpu.VMEM((nc, 1, 128), f32),
            pltpu.VMEM((nc, 16, 128), bf16),
            pltpu.VMEM((b.shape[1], width), bf16),
            dma, dma,
            dma, dma, dma, dma, dma, dma,
            dma, dma((2, nc // 4, WQ)), dma, dma((nc // 2,)),
            dma, dma, dma, dma,
            dma, dma((2, nc // 4, AQ)), dma, dma((nc // 2,)),
        ],
        compiler_params=pltpu.CompilerParams(
            collective_id=0, has_side_effects=True, vmem_limit_bytes=48 * 2**20
        ),
        name="hybrid_block",
    )(x, gt, b, c, ld, skip.reshape(1, heads), w, r, rw, gate)


def solution(mesh):
    in_specs = (
        P("ctx", "exp"),
        P("ctx", "exp"),
        P("ctx", None),
        P("ctx", None),
        P("ctx", "exp"),
        P("exp"),
        P("exp", "ctx"),
        P(),
        P(),
        P("exp", None, "ctx"),
    )
    out_specs = P("exp", None, "ctx")
    return jax.shard_map(body, mesh=mesh, in_specs=in_specs, out_specs=out_specs, check_vma=False)
```

time: 563 us -> 141 us (0.25)
  waiting for transfers between devices: 376 us -> 0 us
  Pallas kernels: 0 us -> 130 us
  local copies, waits for them, and re-layouts: 64.1 us -> 9.2 us
  blocking collectives: 37.3 us -> 0 us
  other arithmetic: 35.1 us -> 0.73 us
  matrix products: 26.7 us -> 0 us
  between operations: 14 us -> 0.03 us
  starting transfers between devices: 6.71 us -> 0 us
    all_gather x3 -> x0, waiting for transfers between devices: 149 us -> none  [the longest x1 70.5 us: body(): gathered = lax.all_gather(mixed_rows, 'ctx', axis=0, tiled=True)]
    pallas_call x0 -> x1, Pallas kernels: none -> 130 us  [body(): pl.pallas_call(kernel, out_shape=jax.ShapeDtypeStruct((1, nc * slots, ff)...]
    all_to_all x1 -> x0, waiting for transfers between devices: 116 us -> none  [body(): lax.all_to_all(outgoing, 'exp', split_axis=1, concat_axis=1, tiled=True)]
    unnamed x5 -> x0, waiting for transfers between devices: 111 us -> none
    reshape x4 -> x0, local copies, waits for them, and re-layouts: 37.4 us -> none  [the longest x2 23.2 us: body(): outgoing.astype(jnp.bfloat16)]
    all_gather x1 -> x0, blocking collectives: 37.3 us -> none  [entering(): lax.all_gather(part.astype(kind), axis)]
    select_n x32 -> x0, other arithmetic: 32.4 us -> none  [step(): return jax.tree.map(lambda a, b: jnp.where(reached, a, b), new, before)]
    dot_general x7 -> x0, matrix products: 26.7 us -> none  [the longest x1 8.9 us: body(): jnp.dot(arrived.reshape(-1, model_width), gate_local, preferred_element_t...]
  transfers between devices with their start and end apart: 5 -> 0, of which waited for: 5 -> 0; matrix products, arithmetic and copies ran while one was open for 10% -> 0% of each run, Pallas kernels for 0% -> 0%
where the time goes in v1:
time: 141 us; the launch traced here: 140 us
  Pallas kernels  130 us (92%)
  local copies, waits for them, and re-layouts  9.2 us (7%)
    pallas_call x1, Pallas kernels, body(): pl.pallas_call(kernel, out_shape=jax.ShapeDtypeStruct((1, nc * slots, ff)...  130 us
    unnamed x18, local copies, waits for them, and re-layouts  9.2 us

profile of v1, /device:TPU:1, one launch (start us, length us, event | category | flops | bytes accessed | tf_op | source)
XLA Modules:
  0.0 140.2 jit_solution(7477181747724552693)
XLA Ops:
  0.0 0.8 copy.17
  0.8 0.7 convert_bitcast_fusion
  1.5 0.8 copy.11.ld_ref
  2.3 0.0 copy-start
  2.3 1.9 %copy-done = bf16[1,4096,384]{2,1,0:T(8,128)(2,1)S(1)} copy-done((bf16[1,4096,384]{2,1,0:T(8,128)(2,1)S(1)}, bf16[1,4096,384]{2,1,0:T(8,128)(2,1)}, u32[]{:S(2)}) %copy-start) | copy-done | bytes 3145752
  4.2 0.0 copy-start.1
  4.2 0.9 copy-done.1
  5.1 0.0 copy-start.2
  5.1 0.9 copy-done.2
  6.0 0.0 copy-start.3
  6.0 0.9 copy-done.3
  6.9 0.0 copy-start.4
  6.9 0.8 copy-done.4
  7.7 0.0 copy-start.5
  7.7 0.8 copy-done.5
  8.4 0.0 copy-start.6
  8.4 0.7 copy-done.6
  9.1 130.2 %hybrid_block.1 = bf16[1,1024,384]{2,1,0:T(8,128)(2,1)S(1)} custom-call(bf16[128,512]{1,0:T(8,128)(2,1)S(1)} %copy-done.1, bf16[128,512]{1,0:T(8,128)(2,1)S(1)} %copy-done.2, bf16[128,128]{1,0:T(8,128)(2,1)S(1)} %copy-done.4, bf16[128,128]{1,0:T(8,128)(2,1)S(1)} %copy-done.5, f32[128,8]{1,0:T(8,128)S(1)} %copy.11.ld_ref, f32[1,8]{1,0:T(1,128)S(1)} %bitcast.14, ...), custom_call_target="tpu_custom_call" | custom-call | tf_op jit(solution)/shard_map/hybrid_block/pallas_call | solution.py:325
  139.3 0.9 copy.19
  (1 shorter events, 0.0 us)
Async XLA Ops:
  2.3 1.9 %copy-start = (bf16[1,4096,384]{2,1,0:T(8,128)(2,1)S(1)}, bf16[1,4096,384]{2,1,0:T(8,128)(2,1)}, u32[]{:S(2)}) copy-start(bf16[1,4096,384]{2,1,0:T(8,128)(2,1)} %g_hbm.1) | copy-start | bytes 9437188
  4.2 0.9 copy-start.1
  5.1 0.9 copy-start.2
  6.0 0.9 copy-start.3
  6.9 0.8 copy-start.4
  7.7 0.8 copy-start.5
  8.4 0.7 copy-start.6

commit v2 on v0

v2 whole, which is shorter than its diff:
```python
import jax
import jax.numpy as jnp
from jax import lax
from jax.experimental import pallas as pl
from jax.experimental.pallas import tpu as pltpu
from jax.sharding import PartitionSpec as P

MESH = pl.DeviceIdType.MESH
SOURCE = 8
CAP = 2
FLOOR = -110.0
HIGHEST = lax.Precision.HIGHEST
WQ = 4
AQ = 4
NEAR = 5
LANES = 128
bf16 = jnp.bfloat16
f32 = jnp.float32


def dot(a, b, dims=((1,), (0,)), precision=None):
    return lax.dot_general(a, b, (dims, ((), ())), preferred_element_type=f32, precision=precision)


def iota(shape, dim):
    return lax.broadcasted_iota(jnp.int32, shape, dim)


def silu(v):
    return v / (1.0 + jnp.exp(-v))


def await_bytes(ref, sem):
    pltpu.make_async_copy(ref, ref, sem).wait()


def kernel(
    x_hbm, gt_hbm, b_hbm, c_hbm, ld_hbm, skip_hbm, w_hbm, r_hbm, rw_hbm, g_hbm,
    out_ref,
    x_ref, gt_ref, b_ref, c_ref, ld_ref, skip_ref, r_ref, rw_ref, gbuf, wbuf, abuf, bbuf, psend, precv, dsend, bsend, mbuf,
    gall, lst, lsib, span, span_sib, stb, dec, rs, rd, pre, ent, goal_ref, value_ref,
    l_sem, l_send, l_recv, s1_send, s1_recv, d1_send, d1_recv, s2_send, s2_recv, e_send, e_recv,
    w_send, w_recv, g_send, g_recv, p_send, p_recv, m_send, m_recv, a_send, a_recv, as_send, as_recv,
    b_send, b_recv, bd_send, bd_recv, bs_send, bs_recv,
):
    nc, ne = lax.axis_size("ctx"), lax.axis_size("exp")
    nz = nc // 2
    up = nz // 2
    c, e = lax.axis_index("ctx"), lax.axis_index("exp")
    z, core = c // 2, c % 2
    tokens, width = x_ref.shape
    heads = ld_ref.shape[0]
    hw = width // heads
    half = width // 2
    slots = tokens // SOURCE * CAP
    sibling = {"ctx": c + 1 - 2 * core}

    def ring(chip):
        return lax.rem(chip + nz, nz)

    def at_z(chip):
        return {"ctx": ring(chip) * 2 + core}

    def remote(src, dst, send, recv, to):
        return pltpu.make_async_remote_copy(src, dst, send, recv, device_id=to, device_id_type=MESH)

    barrier = pltpu.get_barrier_semaphore()
    pl.semaphore_signal(barrier, 1, device_id=sibling, device_id_type=MESH)
    for k in range(1, nz):
        pl.semaphore_signal(barrier, 1, device_id=at_z(z + k), device_id_type=MESH)
    for k in range(1, ne):
        pl.semaphore_signal(barrier, 1, device_id={"exp": lax.rem(e + k, ne)}, device_id_type=MESH)

    pairs_in = (
        (ld_hbm, ld_ref), (x_hbm, x_ref), (b_hbm, b_ref), (c_hbm, c_ref), (skip_hbm, skip_ref), (r_hbm, r_ref), (rw_hbm, rw_ref),
        (gt_hbm, gt_ref),
    )
    loads = [pltpu.make_async_copy(src, dst, l_sem.at[k]) for k, (src, dst) in enumerate(pairs_in)]
    load_w = pltpu.make_async_copy(w_hbm, wbuf.at[z], l_sem.at[8])
    load_g = [pltpu.make_async_copy(g_hbm.at[:, k], gbuf.at[k], l_sem.at[9 + k]) for k in range(2)]
    load_w.start()
    for load in loads + load_g:
        load.start()
    load_w.wait()
    pl.semaphore_wait(barrier, 1 + nz - 1 + ne - 1)

    wrows = wbuf.shape[1] // WQ

    def w_hops(dd, q):
        return up if (q < WQ // 2) == (dd == 0) else up - 1

    def w_piece(chip, q):
        return wbuf.at[ring(chip), pl.ds(q * wrows, wrows), :]

    w_todo = [(i, q) for i in range(up + 1) for q in range(WQ)]

    def tick(n=1):
        for _ in range(n):
            i, q = w_todo.pop(0)
            for dd in range(2):
                turn, hops = 1 - 2 * dd, w_hops(dd, q)
                piece = w_piece(z - turn * i, q)
                if 0 < i <= hops:
                    await_bytes(piece, w_recv.at[dd, i - 1, q])
                if i < hops:
                    remote(piece, piece, w_send, w_recv.at[dd, i, q], at_z(z + turn)).start()

    tick(WQ)

    for load in loads[:3]:
        load.wait()

    ld = jnp.maximum(ld_ref[...], FLOOR)
    row, col = iota((tokens, tokens), 0), iota((tokens, tokens), 1)
    causal = row >= col
    cum = dot(causal.astype(f32), ld, ((1,), (1,)), HIGHEST)
    cum_t = dot(ld, (row <= col).astype(f32), precision=HIGHEST)
    spread = (iota((heads, width), 1) // hw == iota((heads, width), 0)).astype(f32)
    cum_x = dot(cum, spread, precision=HIGHEST)
    x = x_ref[...]
    xf = x.astype(f32)
    to_end = jnp.exp(cum_x[tokens - 1 :, :] - cum_x)
    span[...] = jnp.exp(cum_x[tokens - 1 :, :])
    lst[...] = dot(b_ref[...], (xf * to_end).astype(bf16), ((0,), (0,))).astype(bf16)
    own_state = remote(lst, lsib, l_send.at[0], l_recv.at[0], sibling)
    own_span = remote(span, span_sib, l_send.at[1], l_recv.at[1], sibling)
    own_state.start()
    own_span.start()

    for load in loads[3:]:
        load.wait()
    tick()
    scores = dot(c_ref[...], b_ref[...], ((1,), (1,)))

    def inner(h):
        gap = jnp.minimum(cum[:, h : h + 1] - cum_t[h : h + 1, :], 0.0)
        mixing = (jnp.where(causal, jnp.exp(gap), 0.0) * scores).astype(bf16)
        first_lane = h * hw // LANES * LANES
        return dot(mixing, x[:, first_lane : first_lane + LANES])

    inners = [inner(0)]
    tick()

    own_state.wait_recv()
    own_span.wait_recv()
    mine = pl.ds(pl.multiple_of(core * half, half), half)
    first, second = lst[:, mine].astype(f32), lsib[:, mine].astype(f32)
    decay_own, decay_sib = span[:, mine], span_sib[:, mine]
    is0 = core == 0
    joined = jnp.where(is0, decay_sib, decay_own) * jnp.where(is0, first, second) + jnp.where(is0, second, first)
    joined = joined.astype(bf16)
    lane_blocks = half // LANES
    for j in range(nz):
        rb, lb = j // lane_blocks, j % lane_blocks
        stb[j] = joined[rb * 16 : (rb + 1) * 16, lb * LANES : (lb + 1) * LANES]
    decay = decay_own * decay_sib
    tick()
    for lb in range(lane_blocks):
        dec[lb] = decay[:, lb * LANES : (lb + 1) * LANES]
    for k in range(1, nz):
        j = lax.rem(z + k, nz)
        remote(stb.at[j], rs.at[z], s1_send, s1_recv, at_z(j)).start()
        remote(dec.at[lax.rem(j, lane_blocks)], rd.at[z], d1_send, d1_recv, at_z(j)).start()
    rs[pl.ds(z, 1)] = stb[pl.ds(z, 1)]
    rd[pl.ds(z, 1)] = dec[pl.ds(lax.rem(z, lane_blocks), 1)]

    for h in range(1, 5):
        tick()
        inners.append(inner(h))
    tick()
    await_bytes(rs.at[pl.ds(0, nz - 1)], s1_recv)
    await_bytes(rd.at[pl.ds(0, nz - 1)], d1_recv)
    state = jnp.zeros(rs.shape[1:], f32)
    for j in range(nz):
        if j == nz // 2:
            tick()
        pre[j] = state.astype(bf16)
        state = rd[j] * state + rs[j].astype(f32)
    tick()
    place = (pl.ds(pl.multiple_of(z // lane_blocks * 16, 16), 16), pl.ds(pl.multiple_of(z % lane_blocks * LANES, LANES), LANES))
    for k in range(1, nz):
        j = lax.rem(z + k, nz)
        remote(pre.at[j], ent.at[core, place[0], place[1]], s2_send, s2_recv, at_z(j)).start()
    ent[core, place[0], place[1]] = pre[z]

    for h in range(5, heads):
        tick()
        inners.append(inner(h))
    per = LANES // hw
    pairs = []
    for p in range(width // LANES):
        part = inners[p * per]
        for k in range(1, per):
            part = jnp.where(iota(part.shape, 1) // hw == k, inners[p * per + k], part)
        pairs.append(part)
    tick()
    within = jnp.concatenate(pairs, axis=1) + dot(skip_ref[...], spread, precision=HIGHEST) * xf
    tick()

    before = ((row // SOURCE == col // SOURCE) & (row < col)).astype(bf16)

    def rows_of(ref, k):
        return jnp.concatenate([ref[k : k + 1, j * tokens : (j + 1) * tokens] for j in range(nc)], axis=0)

    own0, own1 = rows_of(r_ref, 0) == e, rows_of(r_ref, 1) == e
    own = own0 | own1
    tick()
    own_pos = dot(own.astype(bf16), before)
    first_slot = (iota((nc, tokens), 1) // SOURCE * CAP).astype(f32)
    goal_ref[...] = jnp.where(own, first_slot + own_pos, -1.0)
    value_ref[...] = jnp.where(own0, rows_of(rw_ref, 0), jnp.where(own1, rows_of(rw_ref, 1), 0.0))

    tick()

    await_bytes(pre.at[pl.ds(0, nz - 1)], s2_recv)
    entering = remote(ent.at[core], ent.at[core], e_send, e_recv, sibling)
    entering.start()
    tick(2)
    await_bytes(ent.at[1 - core], e_recv)
    carried = jnp.concatenate([ent[0], ent[1]], axis=1)
    after0 = (span_sib[...] * carried.astype(f32) + lsib[...].astype(f32)).astype(bf16)
    carried = jnp.where(is0, carried.astype(f32), after0.astype(f32)).astype(bf16)
    tick()
    overall = within + dot(c_ref[...], carried) * jnp.exp(cum_x)
    tick()
    gall[pl.ds(core, 1)] = (overall * silu(gt_ref[...].astype(f32))).astype(bf16)[None]
    both_cores = remote(gall.at[core], gall.at[core], g_send, g_recv, sibling)
    both_cores.start()

    def send_part(part, j):
        @pl.when(j != e)
        def _():
            remote(psend.at[part, j], precv.at[part, e], p_send.at[part], p_recv.at[part], {"exp": j}).start()

    def project(first_chip, count, at_once):
        chips = [ring(first_chip + lax.rem(e + k, count)) for k in range(count)]
        for k in range(0, count, 2):
            some = chips[k : k + 2]
            out = dot(gall[...].reshape(2 * tokens, width), jnp.concatenate([wbuf[j] for j in some], axis=1)).astype(bf16)
            for s, j in enumerate(some):
                for part in range(2):
                    psend[part, j] = out[part * tokens : (part + 1) * tokens, s * LANES : (s + 1) * LANES]
                send_part(0, j)
                if at_once:
                    send_part(1, j)
            tick(min(2, len(w_todo)))
        if not at_once:
            for j in chips:
                send_part(1, j)

    def summed(part):
        precv[part, pl.ds(e, 1)] = psend[part, pl.ds(e, 1)]
        await_bytes(psend.at[part, pl.ds(0, ne - 1)], p_recv.at[part])
        total = precv[part, 0].astype(f32)
        for k in range(1, ne):
            total += precv[part, k].astype(f32)
        return total.astype(bf16)

    tick(max(1, len(w_todo) - WQ * (up - NEAR)))
    await_bytes(gall.at[1 - core], g_recv)
    project(z - NEAR, 2 * NEAR + 1, True)
    tick(len(w_todo))
    project(z + NEAR + 1, nz - 2 * NEAR - 1, False)

    def to_slots(block, values):
        at = pl.ds(pl.multiple_of(block * tokens, tokens), tokens)
        experts = iota((ne, tokens), 0)
        hit = (r_ref[0:1, at] == experts) | (r_ref[1:2, at] == experts)
        pos = dot(hit.astype(bf16), before).astype(jnp.int32)
        target = jnp.where(hit, iota((ne, tokens), 1) // SOURCE * CAP + pos, -1)
        masks = (target[:, None, :] == iota((ne, slots, tokens), 1)).astype(f32).astype(bf16)
        return dot(masks.reshape(ne * slots, tokens), values).astype(bf16).reshape(ne, slots, values.shape[1])

    lane = pl.ds(pl.multiple_of(e * LANES, LANES), LANES)
    dsend[...] = to_slots(z * 2, summed(0))
    for k in range(1, ne):
        j = lax.rem(e + k, ne)
        remote(dsend.at[j], abuf.at[z, core, :, lane], m_send, m_recv, {"exp": j}).start()
    abuf[z, core, :, lane] = dsend[e]

    second_half = summed(1)
    mbuf[0, 0] = second_half
    mbuf[1, 0] = second_half

    def b_ring(i):
        for dd in range(2):
            turn, hops = 1 - 2 * dd, up - dd

            @pl.when((i > 0) & (i <= hops))
            def _():
                await_bytes(mbuf.at[dd, i], b_recv.at[dd, lax.rem(i + up - 1, up)])

            @pl.when(i < hops)
            def _():
                remote(mbuf.at[dd, i], mbuf.at[dd, i + 1], b_send.at[dd], b_recv.at[dd, lax.rem(i, up)], at_z(z + turn)).start()

    def b_dispatch(dd, i):
        chip = ring(z - (1 - 2 * dd) * i)
        bsend[chip] = to_slots(chip * 2 + 1, mbuf[dd, i])

        def one(k, _):
            j = lax.rem(e + k, ne)
            remote(bsend.at[chip, j], bbuf.at[chip, core, :, lane], bd_send, bd_recv.at[chip], {"exp": j}).start()
            return 0

        lax.fori_loop(1, ne, one, 0)
        bbuf[chip, core, :, lane] = bsend[chip, e]

    def b_side(dd, i):
        chip = ring(z - (1 - 2 * dd) * i)
        await_bytes(bsend.at[chip, pl.ds(0, ne - 1)], bd_recv.at[chip])
        block = bbuf.at[chip, core]
        remote(block, block, bs_send, bs_recv.at[chip], sibling).start()

    acols = abuf.shape[3] // AQ

    def a_ring(i, q):
        for dd in range(2):
            turn, hops = 1 - 2 * dd, up if (q < AQ // 2) == (dd == 0) else up - 1
            piece = abuf.at[ring(z - turn * i), core, :, pl.ds(q * acols, acols)]

            @pl.when((i > 0) & (i <= hops))
            def _():
                await_bytes(piece, a_recv.at[dd, lax.rem(i + up - 1, up), q])

            @pl.when(i < hops)
            def _():
                remote(piece, piece, a_send, a_recv.at[dd, lax.rem(i, up), q], at_z(z + turn)).start()

    def a_side(dd, i):
        chip = ring(z - (1 - 2 * dd) * i)
        block = abuf.at[chip, core]
        remote(block, block, as_send, as_recv.at[chip], sibling).start()

    def expert(i):
        chips = (ring(z - i), ring(z + lax.rem(i, up)))
        for chip in chips:
            await_bytes(abuf.at[chip, 1 - core], as_recv.at[chip])
            await_bytes(bbuf.at[chip, 1 - core], bs_recv.at[chip])

        product = None
        for p in range(2):
            rows = jnp.concatenate([buf[chip, p] for chip in chips for buf in (abuf, bbuf)], axis=0)
            part = dot(rows, gbuf[p].reshape(rows.shape[1], gbuf.shape[3]))
            product = part if product is None else product + part
        for k, chip in enumerate(chips):
            weights = []
            for s in range(2):
                goal, value = goal_ref[pl.ds(chip * 2 + s, 1), :], value_ref[pl.ds(chip * 2 + s, 1), :]
                at = goal == iota((slots, tokens), 0).astype(f32)
                weights.append(jnp.sum(jnp.where(at, value, 0.0), axis=1, keepdims=True))
            weight = jnp.concatenate(weights, axis=0)
            part = product[k * 2 * slots : (k + 1) * 2 * slots]
            out_ref[0, pl.ds(pl.multiple_of(chip * 2 * slots, 2 * slots), 2 * slots), :] = (weight * silu(part)).astype(bf16)

    def step(i, _):
        b_ring(i)
        a_ring(i - 1, 0)

        @pl.when(i <= up)
        def _():
            b_dispatch(0, i)

        a_ring(i - 1, 1)

        @pl.when(i < up)
        def _():
            b_dispatch(1, i)

        a_ring(i - 1, 2)

        @pl.when(i <= up + 1)
        def _():
            b_side(0, i - 1)

        @pl.when((i > 1) & (i < up + 1))
        def _():
            b_side(1, i - 1)

        a_ring(i - 1, 3)

        @pl.when(i <= up + 1)
        def _():
            a_side(0, i - 1)

        @pl.when((i > 1) & (i < up + 1))
        def _():
            a_side(1, i - 1)

        @pl.when(i > 2)
        def _():
            expert(i - 2)

        return 0

    b_ring(0)
    b_dispatch(0, 0)
    for load in load_g:
        load.wait()
    await_bytes(dsend.at[pl.ds(0, ne - 1)], m_recv)
    lax.fori_loop(1, up + 3, step, 0)

    own_state.wait_send()
    own_span.wait_send()
    entering.wait_send()
    await_bytes(stb.at[pl.ds(0, nz - 1)], s1_send)
    await_bytes(rd.at[pl.ds(0, nz - 1)], d1_send)
    await_bytes(pre.at[pl.ds(0, nz - 1)], s2_send)
    await_bytes(wbuf.at[pl.ds(0, nz - 1)], w_send)
    both_cores.wait_send()
    for part in range(2):
        await_bytes(psend.at[part, pl.ds(0, ne - 1)], p_send.at[part])
    await_bytes(dsend.at[pl.ds(0, ne - 1)], m_send)
    await_bytes(abuf.at[pl.ds(0, nz - 1), 0], a_send)
    await_bytes(abuf.at[:, 0], as_send)
    for dd in range(2):
        await_bytes(mbuf.at[dd, pl.ds(0, up - dd)], b_send.at[dd])
    await_bytes(bsend.at[:, pl.ds(0, ne - 1)], bd_send)
    await_bytes(bbuf.at[:, 0], bs_send)


def body(x, gt, b, c, ld, skip, w, routes, weights, gate):
    nc, ne = lax.axis_size("ctx"), lax.axis_size("exp")
    nz = nc // 2
    tokens, width = x.shape
    heads = ld.shape[1]
    depth, shard = w.shape
    wide = shard * nc
    slots = tokens // SOURCE * CAP
    ff = gate.shape[2]
    blocks = width // 2 // LANES
    hbm = pl.BlockSpec(memory_space=pl.ANY)
    dma = pltpu.SemaphoreType.DMA
    r = routes.T
    rw = weights.T.astype(f32)

    def vmem(shape, kind=bf16):
        return pltpu.VMEM(shape, kind)

    return pl.pallas_call(
        kernel,
        out_shape=jax.ShapeDtypeStruct((1, nc * slots, ff), bf16),
        in_specs=[hbm] * 10,
        out_specs=pl.BlockSpec(memory_space=pltpu.VMEM),
        scratch_shapes=[
            vmem(x.shape), vmem(gt.shape), vmem(b.shape), vmem(c.shape), vmem((heads, tokens), f32), vmem((1, heads), f32),
            vmem(r.shape, jnp.int32), vmem(rw.shape, f32),
            vmem((2, ne, LANES, ff)), vmem((nz, depth, shard)),
            vmem((nz, 2, slots, wide // 2)), vmem((nz, 2, slots, wide // 2)),
            vmem((2, ne, tokens, LANES)), vmem((2, ne, tokens, LANES)),
            vmem((ne, slots, LANES)), vmem((nz, ne, slots, LANES)), vmem((2, nz // 2 + 1, tokens, LANES)),
            vmem((2, *x.shape)), vmem((b.shape[1], width)), vmem((b.shape[1], width)), vmem((1, width), f32), vmem((1, width), f32),
            vmem((nz, 16, LANES)), vmem((blocks, 1, LANES), f32), vmem((nz, 16, LANES)), vmem((nz, 1, LANES), f32),
            vmem((nz, 16, LANES)), vmem((2, b.shape[1], width // 2)),
            vmem((nc, tokens), f32), vmem((nc, tokens), f32),
            dma((11,)), dma((2,)), dma((2,)), dma, dma, dma, dma, dma, dma, dma, dma,
            dma, dma((2, nz // 2, WQ)), dma, dma,
            dma((2,)), dma((2,)), dma, dma,
            dma, dma((2, nz // 2, AQ)), dma, dma((nz,)),
            dma((2,)), dma((2, nz // 2)), dma, dma((nz,)), dma, dma((nz,)),
        ],
        compiler_params=pltpu.CompilerParams(
            collective_id=0, has_side_effects=True, vmem_limit_bytes=56 * 2**20
        ),
        name="hybrid_block",
    )(x, gt, b, c, ld.T, skip.reshape(1, heads), w, r, rw, gate.reshape(ne, 2, LANES, ff))


def solution(mesh):
    in_specs = (
        P("ctx", "exp"),
        P("ctx", "exp"),
        P("ctx", None),
        P("ctx", None),
        P("ctx", "exp"),
        P("exp"),
        P("exp", "ctx"),
        P(),
        P(),
        P("exp", None, "ctx"),
    )
    out_specs = P("exp", None, "ctx")
    return jax.shard_map(body, mesh=mesh, in_specs=in_specs, out_specs=out_specs, check_vma=False)
```

time: 563 us -> 114 us (0.20)
  waiting for transfers between devices: 376 us -> 0 us
  Pallas kernels: 0 us -> 111 us
  local copies, waits for them, and re-layouts: 64.1 us -> 2.09 us
  blocking collectives: 37.3 us -> 0 us
  other arithmetic: 35.1 us -> 1.34 us
  matrix products: 26.7 us -> 0 us
  between operations: 14 us -> 0.01 us
  starting transfers between devices: 6.71 us -> 0 us
    all_gather x3 -> x0, waiting for transfers between devices: 149 us -> none  [the longest x1 70.5 us: body(): gathered = lax.all_gather(mixed_rows, 'ctx', axis=0, tiled=True)]
    all_to_all x1 -> x0, waiting for transfers between devices: 116 us -> none  [body(): lax.all_to_all(outgoing, 'exp', split_axis=1, concat_axis=1, tiled=True)]
    unnamed x5 -> x0, waiting for transfers between devices: 111 us -> none
    pallas_call x0 -> x1, Pallas kernels: none -> 111 us  [body(): pl.pallas_call(kernel, out_shape=jax.ShapeDtypeStruct((1, nc * slots, ff)...]
    reshape x4 -> x0, local copies, waits for them, and re-layouts: 37.4 us -> none  [the longest x2 23.2 us: body(): outgoing.astype(jnp.bfloat16)]
    all_gather x1 -> x0, blocking collectives: 37.3 us -> none  [entering(): lax.all_gather(part.astype(kind), axis)]
    select_n x32 -> x0, other arithmetic: 32.4 us -> none  [step(): return jax.tree.map(lambda a, b: jnp.where(reached, a, b), new, before)]
    dot_general x7 -> x0, matrix products: 26.7 us -> none  [the longest x1 8.9 us: body(): jnp.dot(arrived.reshape(-1, model_width), gate_local, preferred_element_t...]
  transfers between devices with their start and end apart: 5 -> 0, of which waited for: 5 -> 0; matrix products, arithmetic and copies ran while one was open for 10% -> 0% of each run, Pallas kernels for 0% -> 0%
where the time goes in v2:
time: 114 us
  Pallas kernels  111 us (97%)
  local copies, waits for them, and re-layouts  2.09 us (2%)
  other arithmetic  1.34 us (1%)
    pallas_call x1, Pallas kernels, body(): pl.pallas_call(kernel, out_shape=jax.ShapeDtypeStruct((1, nc * slots, ff)...  111 us

profile of v2, /device:TPU:1, one launch (start us, length us, event | category | flops | bytes accessed | tf_op | source)
XLA Modules:
  0.0 114.1 jit_solution(12170950506717145721)
XLA Ops:
  0.0 1.3 %convert_bitcast_fusion.rw_hbm = f32[2,4096]{1,0:T(2,128)} fusion(bf16[4096,2]{0,1:T(2,128)(2,1)} %param.18), kind=kLoop, calls=%fused_computation | loop fusion | flops 8192 | bytes 49152 | tf_op jit(solution)/shard_map/convert_element_type | solution.py:435
  1.3 110.7 %hybrid_block.1 = bf16[1,1024,384]{2,1,0:T(8,128)(2,1)} custom-call(bf16[128,512]{1,0:T(8,128)(2,1)} %x_hbm.1, bf16[128,512]{1,0:T(8,128)(2,1)} %gt_hbm.1, bf16[128,128]{1,0:T(8,128)(2,1)} %b_hbm.1, bf16[128,128]{1,0:T(8,128)(2,1)} %c_hbm.1, f32[8,128]{1,0:T(8,128)} %bitcast.8, f32[1,8]{1,0:T(1,128)} %bitcast.9, bf16[512,128]{1,0:T(8,128)(2,1)} %w_hbm.1, ...), custom_call_target="tpu_custom_call" | custom-call | tf_op jit(solution)/shard_map/hybrid_block/pallas_call | solution.py:440
  112.0 2.1 %copy.12 = bf16[1,1024,384]{2,1,0:T(8,128)(2,1)} copy(bf16[1,1024,384]{2,1,0:T(8,128)(2,1)} %hybrid_block.1) | data formatting | bytes 1572864

commit v3 on v2

--- a/solution.py
+++ b/solution.py
@@ -12,7 +12,7 @@
 HIGHEST = lax.Precision.HIGHEST
 WQ = 4
 AQ = 4
-NEAR = 5
+NEAR, MIDDLE = 3, 5
 LANES = 128
 bf16 = jnp.bfloat16
 f32 = jnp.float32
@@ -95,7 +95,7 @@
     w_todo = [(i, q) for i in range(up + 1) for q in range(WQ)]
 
     def tick(n=1):
-        for _ in range(n):
+        for _ in range(min(n, len(w_todo))):
             i, q = w_todo.pop(0)
             for dd in range(2):
                 turn, hops = 1 - 2 * dd, w_hops(dd, q)
@@ -232,9 +232,8 @@
         def _():
             remote(psend.at[part, j], precv.at[part, e], p_send.at[part], p_recv.at[part], {"exp": j}).start()
 
-    def project(first_chip, count, at_once):
-        chips = [ring(first_chip + lax.rem(e + k, count)) for k in range(count)]
-        for k in range(0, count, 2):
+    def project(chips, ticks, at_once):
+        for k in range(0, len(chips), 2):
             some = chips[k : k + 2]
             out = dot(gall[...].reshape(2 * tokens, width), jnp.concatenate([wbuf[j] for j in some], axis=1)).astype(bf16)
             for s, j in enumerate(some):
@@ -243,10 +242,13 @@
                 send_part(0, j)
                 if at_once:
                     send_part(1, j)
-            tick(min(2, len(w_todo)))
+            tick(ticks)
         if not at_once:
             for j in chips:
                 send_part(1, j)
+
+    def within_reach(apart):
+        tick(max(0, len(w_todo) - WQ * (up - apart)))
 
     def summed(part):
         precv[part, pl.ds(e, 1)] = psend[part, pl.ds(e, 1)]
@@ -256,11 +258,17 @@
             total += precv[part, k].astype(f32)
         return total.astype(bf16)
 
-    tick(max(1, len(w_todo) - WQ * (up - NEAR)))
     await_bytes(gall.at[1 - core], g_recv)
-    project(z - NEAR, 2 * NEAR + 1, True)
-    tick(len(w_todo))
-    project(z + NEAR + 1, nz - 2 * NEAR - 1, False)
+    count = 2 * NEAR + 1
+    within_reach(NEAR)
+    project([ring(z - NEAR + lax.rem(e + k, count)) for k in range(count)], 2, True)
+    count = 2 * (MIDDLE - NEAR)
+    within_reach(MIDDLE)
+    turns = [lax.rem(e + k, count) for k in range(count)]
+    project([ring(z + (1 - 2 * (t % 2)) * (NEAR + 1 + t // 2)) for t in turns], 2, True)
+    count = nz - 2 * MIDDLE - 1
+    within_reach(up)
+    project([ring(z + MIDDLE + 1 + lax.rem(e + k, count)) for k in range(count)], 0, False)
 
     def to_slots(block, values):
         at = pl.ds(pl.multiple_of(block * tokens, tokens), tokens)
@@ -369,27 +377,27 @@
 
         a_ring(i - 1, 2)
 
+        @pl.when((i > 1) & (i <= up + 2))
+        def _():
+            b_side(0, i - 2)
+
+        @pl.when((i > 2) & (i < up + 2))
+        def _():
+            b_side(1, i - 2)
+
+        a_ring(i - 1, 3)
+
         @pl.when(i <= up + 1)
         def _():
-            b_side(0, i - 1)
+            a_side(0, i - 1)
 
         @pl.when((i > 1) & (i < up + 1))
         def _():
-            b_side(1, i - 1)
-
-        a_ring(i - 1, 3)
-
-        @pl.when(i <= up + 1)
-        def _():
-            a_side(0, i - 1)
-
-        @pl.when((i > 1) & (i < up + 1))
-        def _():
             a_side(1, i - 1)
 
-        @pl.when(i > 2)
-        def _():
-            expert(i - 2)
+        @pl.when(i > 3)
+        def _():
+            expert(i - 3)
 
         return 0
 
@@ -398,7 +406,7 @@
     for load in load_g:
         load.wait()
     await_bytes(dsend.at[pl.ds(0, ne - 1)], m_recv)
-    lax.fori_loop(1, up + 3, step, 0)
+    lax.fori_loop(1, up + 4, step, 0)
 
     own_state.wait_send()
     own_span.wait_send()

time: 114 us -> 113 us (level)
  Pallas kernels: 111 us -> 109 us
    pallas_call x1, Pallas kernels: 111 us -> 109 us  [body(): pl.pallas_call(kernel, out_shape=jax.ShapeDtypeStruct((1, nc * slots, ff)...]
where the time goes in v3:
time: 113 us
  Pallas kernels  109 us (96%)
  local copies, waits for them, and re-layouts  2.09 us (2%)
  other arithmetic  1.34 us (1%)
    pallas_call x1, Pallas kernels, body(): pl.pallas_call(kernel, out_shape=jax.ShapeDtypeStruct((1, nc * slots, ff)...  109 us

profile of v3, /device:TPU:1, one launch (start us, length us, event | category | flops | bytes accessed | tf_op | source)
XLA Modules:
  0.0 112.6 jit_solution(13251622371460276689)
XLA Ops:
  0.0 1.3 %convert_bitcast_fusion.rw_hbm = f32[2,4096]{1,0:T(2,128)} fusion(bf16[4096,2]{0,1:T(2,128)(2,1)} %param.18), kind=kLoop, calls=%fused_computation | loop fusion | flops 8192 | bytes 49152 | tf_op jit(solution)/shard_map/convert_element_type | solution.py:443
  1.3 109.2 %hybrid_block.1 = bf16[1,1024,384]{2,1,0:T(8,128)(2,1)} custom-call(bf16[128,512]{1,0:T(8,128)(2,1)} %x_hbm.1, bf16[128,512]{1,0:T(8,128)(2,1)} %gt_hbm.1, bf16[128,128]{1,0:T(8,128)(2,1)} %b_hbm.1, bf16[128,128]{1,0:T(8,128)(2,1)} %c_hbm.1, f32[8,128]{1,0:T(8,128)} %bitcast.8, f32[1,8]{1,0:T(1,128)} %bitcast.9, bf16[512,128]{1,0:T(8,128)(2,1)} %w_hbm.1, ...), custom_call_target="tpu_custom_call" | custom-call | tf_op jit(solution)/shard_map/hybrid_block/pallas_call | solution.py:448
  110.5 2.1 %copy.12 = bf16[1,1024,384]{2,1,0:T(8,128)(2,1)} copy(bf16[1,1024,384]{2,1,0:T(8,128)(2,1)} %hybrid_block.1) | data formatting | bytes 1572864

commit v4 on v3

--- a/solution.py
+++ b/solution.py
@@ -35,7 +35,7 @@
 
 
 def kernel(
-    x_hbm, gt_hbm, b_hbm, c_hbm, ld_hbm, skip_hbm, w_hbm, r_hbm, rw_hbm, g_hbm,
+    x_hbm, gt_hbm, b_hbm, c_hbm, ld_hbm, skip_hbm, w_hbm, r_hbm, rw_in, g_hbm,
     out_ref,
     x_ref, gt_ref, b_ref, c_ref, ld_ref, skip_ref, r_ref, rw_ref, gbuf, wbuf, abuf, bbuf, psend, precv, dsend, bsend, mbuf,
     gall, lst, lsib, span, span_sib, stb, dec, rs, rd, pre, ent, goal_ref, value_ref,
@@ -72,12 +72,12 @@
         pl.semaphore_signal(barrier, 1, device_id={"exp": lax.rem(e + k, ne)}, device_id_type=MESH)
 
     pairs_in = (
-        (ld_hbm, ld_ref), (x_hbm, x_ref), (b_hbm, b_ref), (c_hbm, c_ref), (skip_hbm, skip_ref), (r_hbm, r_ref), (rw_hbm, rw_ref),
+        (ld_hbm, ld_ref), (x_hbm, x_ref), (b_hbm, b_ref), (c_hbm, c_ref), (skip_hbm, skip_ref), (r_hbm, r_ref),
         (gt_hbm, gt_ref),
     )
     loads = [pltpu.make_async_copy(src, dst, l_sem.at[k]) for k, (src, dst) in enumerate(pairs_in)]
-    load_w = pltpu.make_async_copy(w_hbm, wbuf.at[z], l_sem.at[8])
-    load_g = [pltpu.make_async_copy(g_hbm.at[:, k], gbuf.at[k], l_sem.at[9 + k]) for k in range(2)]
+    load_w = pltpu.make_async_copy(w_hbm, wbuf.at[z], l_sem.at[7])
+    load_g = [pltpu.make_async_copy(g_hbm.at[:, k], gbuf.at[k], l_sem.at[8 + k]) for k in range(2)]
     load_w.start()
     for load in loads + load_g:
         load.start()
@@ -198,6 +198,8 @@
     tick()
 
     before = ((row // SOURCE == col // SOURCE) & (row < col)).astype(bf16)
+
+    rw_ref[...] = rw_in[...].astype(f32)
 
     def rows_of(ref, k):
         return jnp.concatenate([ref[k : k + 1, j * tokens : (j + 1) * tokens] for j in range(nc)], axis=0)
@@ -440,7 +442,7 @@
     hbm = pl.BlockSpec(memory_space=pl.ANY)
     dma = pltpu.SemaphoreType.DMA
     r = routes.T
-    rw = weights.T.astype(f32)
+    rw = weights.T
 
     def vmem(shape, kind=bf16):
         return pltpu.VMEM(shape, kind)
@@ -448,7 +450,7 @@
     return pl.pallas_call(
         kernel,
         out_shape=jax.ShapeDtypeStruct((1, nc * slots, ff), bf16),
-        in_specs=[hbm] * 10,
+        in_specs=[hbm] * 8 + [pl.BlockSpec(memory_space=pltpu.VMEM), hbm],
         out_specs=pl.BlockSpec(memory_space=pltpu.VMEM),
         scratch_shapes=[
             vmem(x.shape), vmem(gt.shape), vmem(b.shape), vmem(c.shape), vmem((heads, tokens), f32), vmem((1, heads), f32),
@@ -461,7 +463,7 @@
             vmem((nz, 16, LANES)), vmem((blocks, 1, LANES), f32), vmem((nz, 16, LANES)), vmem((nz, 1, LANES), f32),
             vmem((nz, 16, LANES)), vmem((2, b.shape[1], width // 2)),
             vmem((nc, tokens), f32), vmem((nc, tokens), f32),
-            dma((11,)), dma((2,)), dma((2,)), dma, dma, dma, dma, dma, dma, dma, dma,
+            dma((10,)), dma((2,)), dma((2,)), dma, dma, dma, dma, dma, dma, dma, dma,
             dma, dma((2, nz // 2, WQ)), dma, dma,
             dma((2,)), dma((2,)), dma, dma,
             dma, dma((2, nz // 2, AQ)), dma, dma((nz,)),

time: 113 us -> 113 us (level)
  other arithmetic: 1.34 us -> 0 us
    convert_element_type x1 -> x0, other arithmetic: 1.34 us -> none  [body(): rw = weights.T.astype(f32)]
    pallas_call x1, Pallas kernels: 109 us -> 110 us  [body(): pl.pallas_call(kernel, out_shape=jax.ShapeDtypeStruct((1, nc * slots, ff)...]
where the time goes in v4:
time: 113 us
  Pallas kernels  110 us (97%)
  local copies, waits for them, and re-layouts  2.09 us (2%)
    pallas_call x1, Pallas kernels, body(): pl.pallas_call(kernel, out_shape=jax.ShapeDtypeStruct((1, nc * slots, ff)...  110 us

profile of v4, /device:TPU:1, one launch (start us, length us, event | category | flops | bytes accessed | tf_op | source)
XLA Modules:
  0.0 112.5 jit_solution(17833506855406857048)
XLA Ops:
  0.0 110.4 %hybrid_block.1 = bf16[1,1024,384]{2,1,0:T(8,128)(2,1)} custom-call(bf16[128,512]{1,0:T(8,128)(2,1)} %x_hbm.1, bf16[128,512]{1,0:T(8,128)(2,1)} %gt_hbm.1, bf16[128,128]{1,0:T(8,128)(2,1)} %b_hbm.1, bf16[128,128]{1,0:T(8,128)(2,1)} %c_hbm.1, f32[8,128]{1,0:T(8,128)} %bitcast.8, f32[1,8]{1,0:T(1,128)} %bitcast.9, bf16[512,128]{1,0:T(8,128)(2,1)} %w_hbm.1, ...), custom_call_target="tpu_custom_call" | custom-call | tf_op jit(solution)/shard_map/hybrid_block/pallas_call | solution.py:450
  110.4 2.1 %copy.12 = bf16[1,1024,384]{2,1,0:T(8,128)(2,1)} copy(bf16[1,1024,384]{2,1,0:T(8,128)(2,1)} %hybrid_block.1) | data formatting | bytes 1572864
